TPU v7x, 128 devices: a whole 4x4x4 slice. The times are simulated.
128 devices in a mesh: edit: 8 (over z, y_hi), seq: 16 (over y_lo, x, core).
Axes of the slice: x: 4, y: 4 (y_hi: 2, y_lo: 2; y = y_hi * 2 + y_lo), z: 4, core: 2. Of those that a mesh axis runs over, the one named last changes fastest.
Arguments:
- projected: bfloat16 [8, 4096, 3, 2048], P('edit', 'seq'), may hold values from -6 to 6
- inject: int32 [8, 16, 16], P('edit', 'seq'), may hold values 0 or 1
- text_kv: bfloat16 [8, 2, 256, 2048], P('edit', None, None, 'seq'), may hold values from -6 to 6
- text_len: int32 [8], P('edit'), may hold values from 64 to 256, as said below
- out_weight: bfloat16 [2048, 3072], replicated, may hold values from -0.125 to 0.125
- gate: float32 [8, 3072], P('edit'), may hold values from 1 to 8
Outputs:
- branch_out: bfloat16 [8, 4096, 3072], P('edit', 'seq')
Inputs may be any that keep to these rules, and one draw needn't show every extreme that they name: `text_len`: in every draw some prompt has all 256 text tokens.
All inputs are finite; a program needn't handle non-finite values. No bound on the sum of `inject` on one device may be relied on, other than what follows from the above.
Results may differ from a plain program's by a relative error of at most 0.0057.
Values may be sent and summed in bfloat16 or wider, within the bound.
A program may use at most 128 MiB of HBM per device.

v0:
```python
import math

import jax
import jax.numpy as jnp
from jax import lax
from jax.sharding import PartitionSpec as P


def broadcast(block, axis, owner):
    block = jnp.where(lax.axis_index(axis) == owner, block, jnp.zeros_like(block))
    return lax.psum(block, axis)


def per_device(projected, inject, text_kv, text_len, out_weight, gate):
    heads_here = inject.shape[1]
    local_width = text_kv.shape[3]
    head_size = local_width // heads_here
    text_rows = text_kv.shape[2]
    tok_rows = projected.shape[1]
    by_heads = lax.all_to_all(projected, "seq", split_axis=3, concat_axis=1, tiled=True)
    source = broadcast(by_heads[:, :, 1:3], "edit", 0)
    total = by_heads.shape[1]
    chosen = (jnp.repeat(inject[0], tok_rows, axis=1).T == 1)[:, None, :, None]
    own_pairs = by_heads[0, :, 1:3].reshape(total, 2, heads_here, head_size)
    source_pairs = source[0].reshape(total, 2, heads_here, head_size)
    pairs = jnp.where(chosen, source_pairs, own_pairs)
    text_pairs = text_kv[0].reshape(2, text_rows, heads_here, head_size)
    all_keys = jnp.concatenate([pairs[:, 0], text_pairs[0]], axis=0)
    values = jnp.concatenate([pairs[:, 1], text_pairs[1]], axis=0)
    usable = jnp.concatenate([jnp.ones((total,), bool), jnp.arange(text_rows) < text_len[0]])
    queries = by_heads[0, :, 0].reshape(total, heads_here, head_size)
    block_rows = min(512, total)
    block_count = total // block_rows
    score_scale = 1.0 / math.sqrt(head_size)

    def attend(query_block):
        scores = (
            jnp.einsum("qhd,khd->hqk", query_block, all_keys, preferred_element_type=jnp.float32)
            * score_scale
        )
        scores = jnp.where(usable[None, None, :], scores, -jnp.inf)
        top_score = jnp.max(scores, axis=2, keepdims=True)
        expo = jnp.exp(scores - top_score)
        weights = (expo / jnp.sum(expo, axis=2, keepdims=True)).astype(jnp.bfloat16)
        return jnp.einsum(
            "hqk,khd->qhd", weights, values, preferred_element_type=jnp.float32
        ).astype(jnp.bfloat16)

    attended = lax.map(attend, queries.reshape(block_count, block_rows, heads_here, head_size))
    attended = attended.reshape(1, total, local_width)
    by_tokens = lax.all_to_all(attended, "seq", split_axis=1, concat_axis=2, tiled=True)
    result = (
        jnp.dot(by_tokens[0], out_weight, preferred_element_type=jnp.float32) * gate[0][None, :]
    )
    return result.astype(jnp.bfloat16)[None]


def solution(mesh):
    return jax.shard_map(
        per_device,
        mesh=mesh,
        in_specs=(
            P("edit", "seq", None, None),
            P("edit", "seq", None),
            P("edit", None, None, "seq"),
            P("edit"),
            P(),
            P("edit", None),
        ),
        out_specs=P("edit", "seq", None),
        check_vma=False,
    )
```

profile of v0, /device:TPU:49, one launch (start us, length us, event | category | flops | bytes accessed | tf_op | source)
XLA Modules:
  0.0 321.0 jit_solution(8679933023806790138)
XLA Ops:
  6.5 7.2 %copy.19 = bf16[1,256,3,2048]{1,2,0,3:T(4,128)(2,1)} copy(bf16[1,256,3,2048]{3,1,2,0:T(8,128)(2,1)} %param.8) | data formatting | bytes 6291456 | tf_op args[0]
  13.7 5.7 %all-to-all-start = ((bf16[1,256,3,2048]{1,2,0,3:T(4,128)(2,1)}), bf16[1,256,3,2048]{1,2,0,3:T(4,128)(2,1)}, u32[]{:S(2)}, u32[]{:S(2)}) async-start(bf16[1,256,3,2048]{1,2,0,3:T(4,128)(2,1)} %copy.19), calls=%async_computation | async-start | bytes 8388608 | tf_op jit(solution)/shard_map/all_to_all | solution.py:20
  19.5 55.9 %all-to-all-done = bf16[1,256,3,2048]{1,2,0,3:T(4,128)(2,1)} async-done(((bf16[1,256,3,2048]{1,2,0,3:T(4,128)(2,1)}), bf16[1,256,3,2048]{1,2,0,3:T(4,128)(2,1)}, u32[]{:S(2)}, u32[]{:S(2)}) %all-to-all-start) | async-done | bytes 3145760 | tf_op jit(solution)/shard_map/all_to_all | solution.py:20
  75.4 5.7 %copy.20 = bf16[1,256,3,16,128]{4,1,3,2,0:T(8,128)(2,1)S(1)} copy(bf16[1,256,3,16,128]{1,2,4,3,0:T(4,128)(2,1)} %bitcast.8) | data formatting | bytes 6291456 | tf_op jit(solution)/shard_map/all_to_all | solution.py:20
  81.2 1.5 select_bitcast_fusion
  84.5 103.0 %all-reduce.3.cloned.1.call-done = bf16[4096,2,1,128]{3,0,1,2:T(8,128)(2,1)} async-done(((bf16[4096,2,1,128]{3,0,1,2:T(8,128)(2,1)}), bf16[4096,2,1,128]{3,0,1,2:T(8,128)(2,1)}) %all-reduce.3.cloned.1.call-update) | async-done | bytes 2097168 | tf_op jit(solution)/shard_map/psum | solution.py:11
  187.5 3.6 %bitcast_select_fusion = bf16[4096,2,1,128]{3,0,1,2:T(8,128)(2,1)S(1)} fusion(bf16[4096,2,1,128]{3,0,1,2:T(8,128)(2,1)} %all-reduce.3.cloned.1.call-done, pred[4096]{0:T(1024)(128)(4,1)S(1)} %eq.25, bf16[1,4096,3,128]{3,1,2,0:T(8,128)(2,1)S(1)} %bitcast.70), kind=kLoop, calls=%fused_computation.16 | loop fusion | flops 1048576 | bytes 6295552 | tf_op jit(solution)/shard_map/jit(_where)/select_n | solution.py:26
  192.6 49.0 %while.10 = (s32[]{:T(128)}, bf16[8,512,1,128]{3,1,2,0:T(8,128)(2,1)S(1)}, pred[4352]{0:T(1024)(128)(4,1)S(1)}, bf16[8,512,1,128]{3,1,2,0:T(8,128)(2,1)}, bf16[4...) while((s32[]{:T(128)}, bf16[8,512,1,128]{3,1,2,0:T(8,128)(2,1)S(1)}, ...), condition=%wide.region_4.5_spmd, body=%wide.region_1.4_spmd.sunk | while | flops 1158740992 | bytes 29244240 | solution.py:49
  192.6 2.4 fusion.20
  194.9 1.4 fusion.21
  196.3 2.4 fusion.22
  198.7 2.4 fusion.20
  201.1 1.4 fusion.21
  202.4 2.4 fusion.22
  204.8 2.4 fusion.20
  208.5 2.4 fusion.22
  210.9 2.4 fusion.20
  214.7 2.4 fusion.22
  217.0 2.4 fusion.20
  219.4 1.4 fusion.21
  220.8 2.4 fusion.22
  223.2 2.4 fusion.20
  225.5 1.4 fusion.21
  226.9 2.4 fusion.22
  229.3 2.4 fusion.20
  233.0 2.4 fusion.22
  235.4 2.4 fusion.20
  239.1 2.4 fusion.22
  241.5 16.7 %copy.26 = bf16[1,4096,128]{2,0,1:T(2,128)(2,1)S(1)} copy(bf16[1,4096,128]{2,1,0:T(8,128)(2,1)S(1)} %bitcast.76) | data formatting | bytes 2097152 | tf_op jit(solution)/shard_map/reshape | solution.py:50
  258.8 22.4 %reduce.4 = bf16[4096,128]{1,0:T(8,128)(2,1)S(1)} reduce(bf16[4096,1,128]{2,1,0:T(2,128)(2,1)S(1)} %bitcast.72, bf16[]{:T(256)} %broadcast.41), dimensions={1}, to_apply=%bitcast.58.reduce_sub_computation | reduce | bytes 2097154
  281.5 21.8 %all_to_all.33 = bf16[16,2,16384]{2,1,0:T(2,128)(2,1)S(1)} all-to-all(bf16[16,2,16384]{2,1,0:T(2,128)(2,1)S(1)} %reshape.82), channel_id=1, replica_groups=mesh['edit'=8,'seq'=16] {'seq'}, dimensions={0} | all-to-all | bytes 2097152 | tf_op jit(solution)/shard_map/all_to_all | solution.py:51
  305.0 9.2 %fusion.11 = bf16[1,256,3072]{2,1,0:T(8,128)(2,1)} fusion(bf16[256,2048]{0,1:T(8,128)(2,1)S(1)} %bitcast.73, bf16[2048,3072]{1,0:T(8,128)(2,1)} %param.12, f32[3072]{0:T(1024)S(1)} %bitcast.77), kind=kOutput, calls=%fused_computation.15 | convolution fusion | flops 3222798336 | bytes 15216640 | tf_op jit(solution)/shard_map/dot_general | solution.py:53
  (29 shorter events, 10.5 us)
Async XLA Ops:
  13.7 61.6 %all-to-all-start = ((bf16[1,256,3,2048]{1,2,0,3:T(4,128)(2,1)}), bf16[1,256,3,2048]{1,2,0,3:T(4,128)(2,1)}, u32[]{:S(2)}, u32[]{:S(2)}) async-start(bf16[1,256,3,2048]{1,2,0,3:T(4,128)(2,1)} %copy.19), calls=%async_computation | async-start | bytes 8388608 | tf_op jit(solution)/shard_map/all_to_all | solution.py:20
  19.4 168.1 %all-reduce.3.cloned.1.call-start = ((), (), s32[]{:S(2)}) async-start(), calls=%async_computation.2 | async-start | bytes 4194304 | tf_op jit(solution)/shard_map/psum | solution.py:11
  81.1 1.5 copy-start.3
  81.1 2.3 copy-start.1
  191.3 1.2 copy-start
  304.3 0.7 copy-start.2
Sparse Core Ops, SparseCore 0:
  82.8 104.7 all-reduce.2
where the time goes:
time: 325 us; the launch traced here: 321 us
  waiting for transfers between devices  159 us (49%)
  matrix products  47.1 us (14%)
  other arithmetic  38.5 us (12%)
  local copies, waits for them, and re-layouts  34.6 us (11%)
  blocking collectives  21.8 us (7%)
  between operations  14.2 us (4%)
  starting transfers between devices  5.74 us (2%)
    psum x1, waiting for transfers between devices, broadcast(): return lax.psum(block, axis)  103 us
    all_to_all x1, waiting for transfers between devices, per_device(): lax.all_to_all(projected, 'seq', split_axis=3, concat_axis=1, tiled=True)  55.9 us
    unnamed x1, other arithmetic  22.4 us
    all_to_all x1, blocking collectives, per_device(): lax.all_to_all(attended, 'seq', split_axis=1, concat_axis=2, tiled=True)  21.8 us
    dot_general x8, matrix products, attend(): jnp.einsum('qhd,khd->hqk', query_block, all_keys, preferred_element_type=...  19 us
    dot_general x8, matrix products, attend(): jnp.einsum('hqk,khd->qhd', weights, values, preferred_element_type=jnp.fl...  18.9 us
    reshape x1, local copies, waits for them, and re-layouts, per_device(): attended = attended.reshape(1, total, local_width)  16.7 us
    reduce_sum x8, other arithmetic, attend(): weights = (expo / jnp.sum(expo, axis=2, keepdims=True)).astype(jnp.bfloat16)  10.9 us
  transfers between devices with their start and end apart: 2, of which 2 were waited for; matrix products, arithmetic and copies ran while one was open for 0% of the time, Pallas kernels for 0%

commit v1 on v0

v1 whole, which is shorter than its diff:
```python
import functools
import math

import jax
import jax.numpy as jnp
from jax import lax
from jax.experimental import pallas as pl
from jax.experimental.pallas import tpu as pltpu
from jax.sharding import PartitionSpec as P

MESH = pl.DeviceIdType.MESH
CONTRACT_LAST = (((1,), (1,)), ((), ()))
LANES = 128


def kernel(
    pieces, edits, ring,
    proj, inj, text, text_len, weight, gate, out,
    own, src, sel, queries, kv, inj_own, inj_all, mask_row,
    s_a, s_b, m_a, m_b, rows_out, cols_out, weight_here,
    load_sem, src_sem, text_sem, weight_sem, inj_send, inj_recv, q_send, q_recv,
    cast_send, cast_recv, kv_send, kv_recv, o_send, o_recv,
):
    e = lax.axis_index("edit")
    me = lax.axis_index("seq")
    z, half = e // 2, e % 2
    depth = edits // 2
    block = own.shape[1]
    rows = block // pieces
    group = rows * ring
    total = block * ring
    text_rows = text.shape[1]
    keys = total + text_rows
    root = e == 0

    def peer(d):
        return lax.rem(me + d, ring)

    def columns(head):
        return pl.ds(pl.multiple_of(head * LANES, LANES), LANES)

    load_own = pltpu.make_async_copy(proj.at[pl.ds(1, 2)], own, load_sem)
    load_own.start()
    load_src = pltpu.make_async_copy(proj.at[pl.ds(1, 2)], src, src_sem)

    @pl.when(root)
    def _():
        load_src.start()

    load_text = pltpu.make_async_copy(
        text, kv.at[:, pl.ds(total, text_rows), pl.ds(0, LANES)], text_sem
    )
    load_text.start()
    load_weight = pltpu.make_async_copy(weight, weight_here, weight_sem)

    barrier = pltpu.get_barrier_semaphore()

    def greet(d, carry):
        pl.semaphore_signal(barrier, inc=1, device_id=(e, peer(d)), device_id_type=MESH)
        return carry

    lax.fori_loop(1, ring, greet, 0)
    up, down = lax.rem(z + 1, depth), lax.rem(z + depth - 1, depth)
    for other in (up * 2 + half, down * 2 + half, z * 2 + 1 - half):
        pl.semaphore_signal(barrier, inc=1, device_id=(other, me), device_id_type=MESH)
    inj_own[...] = jnp.zeros_like(inj_own)
    inj_own[0:1, 0:ring] = inj[...]
    kv[1, :, LANES:] = jnp.ones((keys, LANES), jnp.bfloat16)
    pl.semaphore_wait(barrier, ring - 1 + 3)

    def inj_copy(d):
        return pltpu.make_async_remote_copy(
            inj_own, inj_all.at[me], inj_send, inj_recv, (e, peer(d)), MESH
        )

    def q_copy(d):
        there = peer(d)
        return pltpu.make_async_remote_copy(
            proj.at[0, :, columns(there)],
            queries.at[pl.ds(pl.multiple_of(me * block, block), block)],
            q_send, q_recv, (e, there), MESH,
        )

    def each(first, last, action):
        def step(d, carry):
            action(d)
            return carry

        lax.fori_loop(first, last, step, 0)

    each(1, ring, lambda d: inj_copy(d).start())
    own_inj = pltpu.make_async_copy(inj_own, inj_all.at[me], inj_recv)
    own_inj.start()
    own_q = pltpu.make_async_copy(
        proj.at[0, :, columns(me)],
        queries.at[pl.ds(pl.multiple_of(me * block, block), block)],
        q_recv,
    )
    own_q.start()

    def cast_sends(k):
        odd = lax.rem(k, 2)
        key_from = lax.rem(z - odd + depth, depth)
        value_from = lax.rem(depth - 1 - odd - z + depth, depth)
        first, second = half == 0, half == 1
        return (
            (jnp.logical_or(jnp.logical_and(first, z < depth - 1), jnp.logical_and(second, key_from <= 1)),
             0, up * 2 + half),
            (jnp.logical_or(jnp.logical_and(first, z == odd), jnp.logical_and(second, key_from == 0)),
             0, lax.rem(z + (depth - 1) * half, depth) * 2 + 1),
            (jnp.logical_or(jnp.logical_and(first, z != 1), jnp.logical_and(second, value_from <= 1)),
             1, down * 2 + half),
            (jnp.logical_or(jnp.logical_and(first, z == depth - 1 - odd), jnp.logical_and(second, value_from == 0)),
             1, lax.rem(z + half, depth) * 2 + 1),
        )

    def piece_rows(k):
        return pl.ds(pl.multiple_of(k * rows, rows), rows)

    def cast_copy(k, role, part, there):
        here = src.at[part, piece_rows(k)]
        return pltpu.make_async_remote_copy(
            here, here, cast_send.at[role, k], cast_recv.at[part, k], (there, me), MESH
        )

    def kv_rows(k, owner):
        return pl.ds(pl.multiple_of(k * group + owner * rows, rows), rows)

    def kv_copy(k, d):
        there = peer(d)
        return pltpu.make_async_remote_copy(
            sel.at[:, piece_rows(k), columns(there)],
            kv.at[:, kv_rows(k, me), pl.ds(0, LANES)],
            kv_send.at[k], kv_recv.at[k], (e, there), MESH,
        )

    def own_kv_copy(k):
        return pltpu.make_async_copy(
            sel.at[:, piece_rows(k), columns(me)],
            kv.at[:, kv_rows(k, me), pl.ds(0, LANES)],
            kv_recv.at[k],
        )

    @pl.when(root)
    def _():
        load_src.wait()

    load_own.wait()
    pltpu.make_async_copy(inj_all, inj_all, inj_recv).wait()
    lane = lax.broadcasted_iota(jnp.int32, (1, LANES), 1)
    for head in range(ring):
        mine = jnp.where(lane == me, inj_all[head, 0:1, :], 0)
        taken = jnp.sum(mine, axis=1, keepdims=True)
        mask_row[:, head * LANES : (head + 1) * LANES] = jnp.broadcast_to(taken, (8, LANES))

    q_step = -(-(ring - 1) // pieces)

    def send_piece(k, carry):
        for part in range(2):

            @pl.when(jnp.logical_not(root))
            def _():
                cast_copy(k, 0, part, e).wait_recv()

            for role, (wanted, moved, there) in enumerate(cast_sends(k)):
                if moved == part:

                    @pl.when(wanted)
                    def _(role=role, there=there):
                        cast_copy(k, role, part, there).start()

        here = piece_rows(k)
        taken = mask_row[0:1, :] == 1
        for part in range(2):
            sel[part, here, :] = jnp.where(
                taken, src[part, here, :].astype(jnp.float32), own[part, here, :].astype(jnp.float32)
            ).astype(jnp.bfloat16)
        each(1, ring, lambda d: kv_copy(k, d).start())
        own_kv_copy(k).start()
        for extra in range(q_step):
            d = k * q_step + 1 + extra

            @pl.when(d < ring)
            def _(d=d):
                q_copy(d).start()

        return carry

    lax.fori_loop(0, pieces, send_piece, 0)
    load_weight.start()

    load_text.wait()
    pltpu.make_async_copy(queries, queries, q_recv).wait()

    def await_piece(k, carry):
        part = kv.at[:, pl.ds(pl.multiple_of(k * group, group), group), pl.ds(0, LANES)]
        pltpu.make_async_copy(part, part, kv_recv.at[k]).wait()
        return carry

    lax.fori_loop(0, pieces, await_piece, 0)

    scale = math.log2(math.e) / math.sqrt(LANES)
    chunk = text_rows
    usable = lax.broadcasted_iota(jnp.int32, (1, chunk), 1) < text_len[0]
    scores, tops = (s_a, s_b), (m_a, m_b)

    def at(i):
        owner = lax.rem(me + 1 + i, ring)
        return owner, pl.ds(pl.multiple_of(owner * block, block), block)

    def o_copy(i):
        owner, here = at(i)
        return pltpu.make_async_remote_copy(
            rows_out.at[here], cols_out.at[:, columns(me)], o_send, o_recv, (e, owner), MESH
        )

    def attend(i, slot, first=False, last=False):
        other = 1 - slot
        if not last:
            query = queries[at(i)[1], :]
        if not first:
            top = tops[other][:, 0:1]
        highest, total_out = None, None
        for j in range(keys // chunk):
            here = slice(j * chunk, (j + 1) * chunk)
            if not last:
                s = lax.dot_general(
                    query, kv[0, here, 0:LANES], CONTRACT_LAST, preferred_element_type=jnp.float32
                )
                if j == keys // chunk - 1:
                    s = jnp.where(usable, s, -1e30)
                scores[slot][:, here] = s
                for c in range(chunk // LANES):
                    part = s[:, c * LANES : (c + 1) * LANES]
                    highest = part if highest is None else jnp.maximum(highest, part)
            if not first:
                p = jnp.exp2(scores[other][:, here] * scale - top).astype(jnp.bfloat16)
                part = jnp.dot(p, kv[1, here, :], preferred_element_type=jnp.float32)
                total_out = part if total_out is None else total_out + part
        if not last:
            tops[slot][...] = jnp.broadcast_to(
                jnp.max(highest, axis=1, keepdims=True) * scale, (block, LANES)
            )
        if not first:
            result = total_out[:, :LANES] / total_out[:, LANES : LANES + 1]
            rows_out[at(i - 1)[1], :] = result.astype(jnp.bfloat16)

    def two(h, carry):
        attend(2 * h + 1, 1)
        o_copy(2 * h).start()
        attend(2 * h + 2, 0)
        o_copy(2 * h + 1).start()
        return carry

    attend(0, 0, first=True)
    lax.fori_loop(0, (ring - 2) // 2, two, 0)
    attend(ring - 1, 1)
    o_copy(ring - 2).start()
    attend(ring, 0, last=True)
    own_o = pltpu.make_async_copy(rows_out.at[at(ring - 1)[1]], cols_out.at[:, columns(me)], o_recv)
    own_o.start()
    load_weight.wait()
    pltpu.make_async_copy(cols_out, cols_out, o_recv).wait()

    wide = 512 if out.shape[1] % 512 == 0 else LANES

    def project(n, carry):
        here = pl.ds(pl.multiple_of(n * wide, wide), wide)
        result = jnp.dot(cols_out[...], weight_here[:, here], preferred_element_type=jnp.float32)
        out[:, here] = (result * gate[:, here]).astype(jnp.bfloat16)
        return carry

    lax.fori_loop(0, out.shape[1] // wide, project, 0)

    each(1, ring, lambda d: inj_copy(d).wait_send())
    each(1, ring, lambda d: q_copy(d).wait_send())
    each(0, ring - 1, lambda i: o_copy(i).wait_send())

    def finish_piece(k, carry):
        for role, (wanted, part, there) in enumerate(cast_sends(k)):

            @pl.when(wanted)
            def _(role=role, part=part, there=there):
                cast_copy(k, role, part, there).wait_send()

        each(1, ring, lambda d: kv_copy(k, d).wait_send())
        return carry

    lax.fori_loop(0, pieces, finish_piece, 0)


def per_device(pieces, edits, ring, projected, inject, text_kv, text_len, out_weight, gate):
    block, width = projected.shape[1], projected.shape[3]
    text_rows = text_kv.shape[2]
    total = block * ring
    keys = total + text_rows
    wide = out_weight.shape[1]
    bf16, f32, i32 = jnp.bfloat16, jnp.float32, jnp.int32
    vmem = pl.BlockSpec(memory_space=pltpu.VMEM)
    far = pl.BlockSpec(memory_space=pl.ANY)
    dma = pltpu.SemaphoreType.DMA
    result = pl.pallas_call(
        functools.partial(kernel, pieces, edits, ring),
        out_shape=jax.ShapeDtypeStruct((block, wide), bf16),
        in_specs=[far, vmem, far, pl.BlockSpec(memory_space=pltpu.SMEM), far, vmem],
        out_specs=vmem,
        scratch_shapes=[
            pltpu.VMEM((2, block, width), bf16),
            pltpu.VMEM((2, block, width), bf16),
            pltpu.VMEM((2, block, width), bf16),
            pltpu.VMEM((total, LANES), bf16),
            pltpu.VMEM((2, keys, 2 * LANES), bf16),
            pltpu.VMEM((8, LANES), i32),
            pltpu.VMEM((ring, 8, LANES), i32),
            pltpu.VMEM((8, width), i32),
            pltpu.VMEM((block, keys), f32),
            pltpu.VMEM((block, keys), f32),
            pltpu.VMEM((block, LANES), f32),
            pltpu.VMEM((block, LANES), f32),
            pltpu.VMEM((total, LANES), bf16),
            pltpu.VMEM((block, width), bf16),
            pltpu.VMEM(out_weight.shape, bf16),
            dma, dma, dma, dma, dma, dma, dma, dma,
            dma((4, pieces)), dma((2, pieces)), dma((pieces,)), dma((pieces,)),
            dma, dma,
        ],
        compiler_params=pltpu.CompilerParams(
            collective_id=0, has_side_effects=True, vmem_limit_bytes=56 * 2**20
        ),
    )(
        projected[0].transpose(1, 0, 2), inject[0], text_kv[0], text_len, out_weight, gate,
    )
    return result[None]


def solution(mesh):
    edits, ring = mesh.shape["edit"], mesh.shape["seq"]
    return jax.shard_map(
        functools.partial(per_device, 8, edits, ring),
        mesh=mesh,
        in_specs=(
            P("edit", "seq", None, None),
            P("edit", "seq", None),
            P("edit", None, None, "seq"),
            P("edit"),
            P(),
            P("edit", None),
        ),
        out_specs=P("edit", "seq", None),
        check_vma=False,
    )
```

time: 325 us -> 199 us (0.61)
  the two profiles are of different devices: /device:TPU:49 before, /device:TPU:19 now
where the time goes in v1:
time: 199 us
  Pallas kernels  196 us (98%)
  local copies, waits for them, and re-layouts  2.65 us (1%)
    pallas_call x1, Pallas kernels, per_device(): pl.pallas_call(functools.partial(kernel, pieces, edits, ring), out_shape=...  196 us

profile of v1, /device:TPU:19, one launch (start us, length us, event | category | flops | bytes accessed | tf_op | source)
XLA Modules:
  0.0 199.1 jit_solution(11099796420188488061)
XLA Ops:
  0.7 195.8 %shard_map.64 = bf16[256,3072]{1,0:T(8,128)(2,1)} custom-call(bf16[3,256,2048]{2,1,0:T(8,128)(2,1)} %bitcast.7, s32[1,16]{1,0:T(1,128)} %bitcast.9, bf16[2,256,128]{2,1,0:T(8,128)(2,1)} %bitcast.8, s32[1]{0:T(128)S(6)} %copy.8.text_len, bf16[2048,3072]{1,0:T(8,128)(2,1)} %weight.1, f32[1,3072]{1,0:T(1,128)} %gate.1), custom_call_target="tpu_custom_call" | custom-call | tf_op jit(solution)/shard_map/pallas_call | solution.py:302
  196.4 2.7 %copy.9 = bf16[1,256,3072]{2,1,0:T(8,128)(2,1)} copy(bf16[1,256,3072]{2,1,0:T(8,128)(2,1)} %bitcast.6) | data formatting | bytes 3145728

commit v2 on v0

v2 whole, which is shorter than its diff:
```python
import functools
import math

import jax
import jax.numpy as jnp
from jax import lax
from jax.experimental import pallas as pl
from jax.experimental.pallas import tpu as pltpu
from jax.sharding import PartitionSpec as P

MESH = pl.DeviceIdType.MESH
CONTRACT_LAST = (((1,), (1,)), ((), ()))
LANES = 128
HOP = 2
AHEAD = 3
PIECES = 16


def kernel(
    edits, ring,
    proj, inj, text, text_len, weight, gate, out,
    queries, kv, src, inj_own, inj_here, mask, s_a, s_b, m_a, m_b, rows_out, cols_out, weight_here,
    weight_sem, text_send, text_recv, inj_send, inj_recv, q_send, q_recv,
    cast_send, cast_recv, kv_send, kv_recv, o_send, o_recv,
):
    e = lax.axis_index("edit")
    me = lax.axis_index("seq")
    z, half = e // 2, e % 2
    depth = edits // 2
    block = out.shape[0]
    rows = block // PIECES
    group = rows * ring
    total = block * ring
    text_rows = text.shape[1]
    keys = total + text_rows
    root = e == 0
    swap = ring // 2
    other_row = lax.rem(me + swap, ring)

    def peer(d):
        return lax.rem(me + d, ring)

    def head_of(device):
        return lax.rem(device + swap * half, ring)

    def columns(head):
        return pl.ds(pl.multiple_of(head * LANES, LANES), LANES)

    def each(first, last, action):
        def step(d, carry):
            action(d)
            return carry

        lax.fori_loop(first, last, step, 0)

    load_weight = pltpu.make_async_copy(weight, weight_here, weight_sem)
    load_weight.start()

    barrier = pltpu.get_barrier_semaphore()

    def greet(d):
        pl.semaphore_signal(barrier, inc=1, device_id=(e, peer(d)), device_id_type=MESH)

    each(1, ring, greet)
    up, down = lax.rem(z + 1, depth), lax.rem(z + depth - 1, depth)
    for other in ((up * 2 + half, me), (down * 2 + half, me), (z * 2 + 1 - half, other_row)):
        pl.semaphore_signal(barrier, inc=1, device_id=other, device_id_type=MESH)
    inj_own[...] = jnp.zeros_like(inj_own)
    inj_own[0:1, 0:ring] = inj[...]
    kv[1, :, LANES:] = jnp.ones((keys, LANES), jnp.bfloat16)
    pl.semaphore_wait(barrier, ring - 1 + 3)

    def piece_rows(k):
        return pl.ds(pl.multiple_of(k * rows, rows), rows)

    def group_rows(k):
        return pl.ds(pl.multiple_of(k * group, group), group)

    def landing(k):
        return pl.ds(pl.multiple_of(k * group + me * rows, rows), rows)

    def q_copy(k, d):
        there = peer(d)
        return pltpu.make_async_remote_copy(
            proj.at[0, piece_rows(k), columns(head_of(there))], queries.at[landing(k)],
            q_send, q_recv.at[k], (e, there), MESH,
        )

    def kv_copy(k, d):
        there = peer(d)
        return pltpu.make_async_remote_copy(
            proj.at[pl.ds(1, 2), piece_rows(k), columns(head_of(there))],
            kv.at[:, landing(k), pl.ds(0, LANES)],
            kv_send, kv_recv.at[k], (e, there), MESH,
        )

    def push_q(k):
        each(1, ring, lambda d: q_copy(k, d).start())
        pltpu.make_async_copy(
            proj.at[0, piece_rows(k), columns(head_of(me))], queries.at[landing(k)], q_recv.at[k]
        ).start()

    def push_kv(k):
        each(1, ring, lambda d: kv_copy(k, d).start())
        pltpu.make_async_copy(
            proj.at[pl.ds(1, 2), piece_rows(k), columns(head_of(me))],
            kv.at[:, landing(k), pl.ds(0, LANES)], kv_recv.at[k],
        ).start()

    def await_kv(k):
        here = kv.at[:, group_rows(k), pl.ds(0, LANES)]
        pltpu.make_async_copy(here, here, kv_recv.at[k]).wait()

    def near(distance):
        return distance - 2 * (distance // (depth - 1))

    def apart(part, odd):
        if part == 0:
            return lax.rem(z - odd + depth, depth)
        return lax.rem(2 * depth - odd - z, depth)

    def lag(part, odd):
        straight = z if part == 0 else lax.rem(depth - z, depth)
        return HOP * ((1 - half) * straight + half * (odd + 1 + near(apart(part, odd))))

    def cast_sends(part, odd):
        first, second = half == 0, half == 1
        distance = apart(part, odd)
        onward = z < depth - 1 if part == 0 else z != 1
        cross = z == odd if part == 0 else z == lax.rem(depth - odd, depth)
        back = lax.rem(z + (depth - 1) * half, depth) if part == 0 else lax.rem(z + half, depth)
        ahead = up if part == 0 else down
        return (
            (jnp.logical_or(jnp.logical_and(first, onward), jnp.logical_and(second, distance <= 1)),
             (ahead * 2 + half, me)),
            (jnp.logical_or(jnp.logical_and(first, cross), jnp.logical_and(second, distance == 0)),
             (back * 2 + 1, lax.rem(me + swap * (1 - half), ring))),
        )

    def cast_copy(k, role, part, there, first):
        here = kv.at[part, group_rows(k), pl.ds(0, LANES)] if first else src.at[part, group_rows(k)]
        return pltpu.make_async_remote_copy(
            here, src.at[part, group_rows(k)], cast_send.at[2 * part + role, k],
            cast_recv.at[part, k], there, MESH,
        )

    def cast_start(k, part, odd, first):
        for role, (wanted, there) in enumerate(cast_sends(part, odd)):

            @pl.when(wanted)
            def _(role=role, there=there):
                cast_copy(k, role, part, there, first).start()

    def cast_done(k, part, odd):
        for role, (wanted, there) in enumerate(cast_sends(part, odd)):

            @pl.when(wanted)
            def _(role=role, there=there):
                cast_copy(k, role, part, there, False).wait_send()

    most = HOP * depth

    def cast_step(t, carry):
        for odd in range(2):
            for part in range(2):
                k = t - lag(part, odd)
                here = jnp.logical_and(
                    jnp.logical_and(k >= 0, k < PIECES), lax.rem(k + 2 * most, 2) == odd
                )

                @pl.when(jnp.logical_and(here, root))
                def _(k=k, part=part, odd=odd):
                    if part == 0:
                        await_kv(k)
                    cast_start(k, part, odd, True)

                @pl.when(jnp.logical_and(here, jnp.logical_not(root)))
                def _(k=k, part=part, odd=odd):
                    cast_copy(k, 0, part, (e, me), False).wait_recv()
                    cast_start(k, part, odd, False)

        @pl.when(root)
        def _():
            ahead = t + AHEAD

            @pl.when(ahead < PIECES)
            def _():
                push_kv(ahead)

            @pl.when(jnp.logical_and(ahead >= PIECES, ahead < PIECES + PIECES // 2))
            def _():
                push_q(2 * (ahead - PIECES))
                push_q(2 * (ahead - PIECES) + 1)

        @pl.when(jnp.logical_not(root))
        def _():
            quick = PIECES // 4

            @pl.when(t < quick)
            def _():
                each(4 * t, 4 * t + 4, push_q)

            @pl.when(jnp.logical_and(t >= quick, t < quick + PIECES))
            def _():
                push_kv(t - quick)

        return carry

    @pl.when(root)
    def _():
        each(0, AHEAD, push_kv)

    text_here = kv.at[:, pl.ds(total, text_rows), pl.ds(0, LANES)]
    text_copy = pltpu.make_async_remote_copy(text, text_here, text_send, text_recv, (e, other_row), MESH)
    inj_copy = pltpu.make_async_remote_copy(inj_own, inj_here, inj_send, inj_recv, (e, other_row), MESH)

    @pl.when(half == 1)
    def _():
        inj_copy.start()
        text_copy.start()

    @pl.when(half == 0)
    def _():
        pltpu.make_async_copy(inj_own, inj_here, inj_recv).start()
        pltpu.make_async_copy(text, text_here, text_recv).start()

    lax.fori_loop(0, PIECES + most, cast_step, 0)

    inj_copy.wait_recv()
    text_copy.wait_recv()

    @pl.when(jnp.logical_not(root))
    def _():
        lane = lax.broadcasted_iota(jnp.int32, (1, LANES), 1)
        for owner in range(ring):
            taken = jnp.sum(jnp.where(lane == owner, inj_here[0:1, :], 0), axis=1, keepdims=True)
            mask[owner * rows : (owner + 1) * rows, :] = jnp.broadcast_to(taken, (rows, LANES))

        def choose(k):
            await_kv(k)
            here = group_rows(k)
            for part in range(2):
                kv[part, here, 0:LANES] = jnp.where(
                    mask[...] == 1,
                    src[part, here, :].astype(jnp.float32),
                    kv[part, here, 0:LANES].astype(jnp.float32),
                ).astype(jnp.bfloat16)

        each(0, PIECES, choose)

    scale = math.log2(math.e) / math.sqrt(LANES)
    chunk = text_rows
    usable = lax.broadcasted_iota(jnp.int32, (1, chunk), 1) < text_len[0]
    scores, tops = (s_a, s_b), (m_a, m_b)

    def o_copy(k, d):
        there = peer(d)
        return pltpu.make_async_remote_copy(
            rows_out.at[pl.ds(pl.multiple_of(k * group + there * rows, rows), rows)],
            cols_out.at[piece_rows(k), columns(head_of(me))],
            o_send, o_recv, (e, there), MESH,
        )

    def push_o(k):
        each(1, ring, lambda d: o_copy(k, d).start())
        pltpu.make_async_copy(
            rows_out.at[landing(k)], cols_out.at[piece_rows(k), columns(head_of(me))], o_recv
        ).start()

    def attend(i, slot, first=False, last=False):
        other = 1 - slot
        if not last:
            here = queries.at[group_rows(i)]
            pltpu.make_async_copy(here, here, q_recv.at[i]).wait()
            query = queries[group_rows(i), :]
        if not first:
            top = tops[other][:, 0:1]
        highest, total_out = None, None
        for j in range(keys // chunk):
            here = slice(j * chunk, (j + 1) * chunk)
            if not last:
                s = lax.dot_general(
                    query, kv[0, here, 0:LANES], CONTRACT_LAST, preferred_element_type=jnp.float32
                )
                if j == keys // chunk - 1:
                    s = jnp.where(usable, s, -1e30)
                scores[slot][:, here] = s
                for c in range(chunk // LANES):
                    part = s[:, c * LANES : (c + 1) * LANES]
                    highest = part if highest is None else jnp.maximum(highest, part)
            if not first:
                p = jnp.exp2(scores[other][:, here] * scale - top).astype(jnp.bfloat16)
                part = jnp.dot(p, kv[1, here, :], preferred_element_type=jnp.float32)
                total_out = part if total_out is None else total_out + part
        if not last:
            tops[slot][...] = jnp.broadcast_to(
                jnp.max(highest, axis=1, keepdims=True) * scale, (group, LANES)
            )
        if not first:
            result = total_out[:, :LANES] / total_out[:, LANES : LANES + 1]
            rows_out[group_rows(i - 1), :] = result.astype(jnp.bfloat16)

    def two(h):
        attend(2 * h + 1, 1)
        push_o(2 * h)
        attend(2 * h + 2, 0)
        push_o(2 * h + 1)

    attend(0, 0, first=True)
    each(0, (PIECES - 2) // 2, two)
    attend(PIECES - 1, 1)
    push_o(PIECES - 2)
    attend(PIECES, 0, last=True)
    push_o(PIECES - 1)
    load_weight.wait()
    pltpu.make_async_copy(cols_out, cols_out, o_recv).wait()

    wide = 512 if out.shape[1] % 512 == 0 else LANES

    def project(n):
        here = pl.ds(pl.multiple_of(n * wide, wide), wide)
        result = jnp.dot(cols_out[...], weight_here[:, here], preferred_element_type=jnp.float32)
        out[:, here] = (result * gate[:, here]).astype(jnp.bfloat16)

    each(0, out.shape[1] // wide, project)

    @pl.when(half == 1)
    def _():
        inj_copy.wait_send()
        text_copy.wait_send()

    def finish_piece(k):
        for odd in range(2):

            @pl.when(lax.rem(k, 2) == odd)
            def _(odd=odd):
                for part in range(2):
                    cast_done(k, part, odd)

        each(1, ring, lambda d: q_copy(k, d).wait_send())
        each(1, ring, lambda d: kv_copy(k, d).wait_send())
        each(1, ring, lambda d: o_copy(k, d).wait_send())

    each(0, PIECES, finish_piece)


def per_device(edits, ring, projected, inject, text_kv, text_len, out_weight, gate):
    block, width = projected.shape[1], projected.shape[3]
    text_rows = text_kv.shape[2]
    total = block * ring
    keys = total + text_rows
    group = total // PIECES
    bf16, f32, i32 = jnp.bfloat16, jnp.float32, jnp.int32
    vmem = pl.BlockSpec(memory_space=pltpu.VMEM)
    far = pl.BlockSpec(memory_space=pl.ANY)
    dma = pltpu.SemaphoreType.DMA
    result = pl.pallas_call(
        functools.partial(kernel, edits, ring),
        out_shape=jax.ShapeDtypeStruct((block, out_weight.shape[1]), bf16),
        in_specs=[far, vmem, far, pl.BlockSpec(memory_space=pltpu.SMEM), far, vmem],
        out_specs=vmem,
        scratch_shapes=[
            pltpu.VMEM((total, LANES), bf16),
            pltpu.VMEM((2, keys, 2 * LANES), bf16),
            pltpu.VMEM((2, total, LANES), bf16),
            pltpu.VMEM((8, LANES), i32),
            pltpu.VMEM((8, LANES), i32),
            pltpu.VMEM((group, LANES), i32),
            pltpu.VMEM((group, keys), f32),
            pltpu.VMEM((group, keys), f32),
            pltpu.VMEM((group, LANES), f32),
            pltpu.VMEM((group, LANES), f32),
            pltpu.VMEM((total, LANES), bf16),
            pltpu.VMEM((block, width), bf16),
            pltpu.VMEM(out_weight.shape, bf16),
            dma, dma, dma, dma, dma, dma, dma((PIECES,)),
            dma((4, PIECES)), dma((2, PIECES)), dma, dma((PIECES,)), dma, dma,
        ],
        compiler_params=pltpu.CompilerParams(
            collective_id=0, has_side_effects=True, vmem_limit_bytes=56 * 2**20
        ),
    )(
        projected[0].transpose(1, 0, 2), inject[0], text_kv[0], text_len, out_weight, gate,
    )
    return result[None]


def solution(mesh):
    return jax.shard_map(
        functools.partial(per_device, mesh.shape["edit"], mesh.shape["seq"]),
        mesh=mesh,
        in_specs=(
            P("edit", "seq", None, None),
            P("edit", "seq", None),
            P("edit", None, None, "seq"),
            P("edit"),
            P(),
            P("edit", None),
        ),
        out_specs=P("edit", "seq", None),
        check_vma=False,
    )
```

time: 325 us -> 99.3 us (0.31); the launches traced: 321 us -> 99.1 us
  waiting for transfers between devices: 159 us -> 0 us
  Pallas kernels: 0 us -> 95.8 us
  matrix products: 47.1 us -> 0 us
  other arithmetic: 38.5 us -> 0 us
  local copies, waits for them, and re-layouts: 34.6 us -> 2.65 us
  blocking collectives: 21.8 us -> 0 us
  between operations: 14.2 us -> 0.66 us
  starting transfers between devices: 5.74 us -> 0 us
    psum x1 -> x0, waiting for transfers between devices: 103 us -> none  [broadcast(): return lax.psum(block, axis)]
    pallas_call x0 -> x1, Pallas kernels: none -> 95.8 us  [per_device(): pl.pallas_call(functools.partial(kernel, edits, ring), out_shape=jax.Shap...]
    all_to_all x1 -> x0, waiting for transfers between devices: 55.9 us -> none  [per_device(): lax.all_to_all(projected, 'seq', split_axis=3, concat_axis=1, tiled=True)]
    dot_general x17 -> x0, matrix products: 47.1 us -> none  [the longest x8 19 us: attend(): jnp.einsum('qhd,khd->hqk', query_block, all_keys, preferred_element_type=...]
    unnamed x1 -> x0, other arithmetic: 22.4 us -> none
    all_to_all x1 -> x0, blocking collectives: 21.8 us -> none  [per_device(): lax.all_to_all(attended, 'seq', split_axis=1, concat_axis=2, tiled=True)]
    reshape x1 -> x0, local copies, waits for them, and re-layouts: 16.7 us -> none  [per_device(): attended = attended.reshape(1, total, local_width)]
    reduce_sum x8 -> x0, other arithmetic: 10.9 us -> none  [attend(): weights = (expo / jnp.sum(expo, axis=2, keepdims=True)).astype(jnp.bfloat16)]
  transfers between devices with their start and end apart: 2 -> 0, of which waited for: 2 -> 0; matrix products, arithmetic and copies ran while one was open for 0% -> 0% of each run, Pallas kernels for 0% -> 0%
where the time goes in v2:
time: 99.3 us; the launch traced here: 99.1 us
  Pallas kernels  95.8 us (96%)
  local copies, waits for them, and re-layouts  2.65 us (3%)
    pallas_call x1, Pallas kernels, per_device(): pl.pallas_call(functools.partial(kernel, edits, ring), out_shape=jax.Shap...  95.8 us
    unnamed x1, local copies, waits for them, and re-layouts  2.65 us

profile of v2, /device:TPU:49, one launch (start us, length us, event | category | flops | bytes accessed | tf_op | source)
XLA Modules:
  0.0 99.1 jit_solution(7761100785752392821)
XLA Ops:
  0.7 95.8 %shard_map.64 = bf16[256,3072]{1,0:T(8,128)(2,1)} custom-call(bf16[3,256,2048]{2,1,0:T(8,128)(2,1)} %bitcast.7, s32[1,16]{1,0:T(1,128)} %bitcast.9, bf16[2,256,128]{2,1,0:T(8,128)(2,1)} %bitcast.8, s32[1]{0:T(128)S(6)} %copy.8.text_len, bf16[2048,3072]{1,0:T(8,128)(2,1)} %weight.1, f32[1,3072]{1,0:T(1,128)} %gate.1), custom_call_target="tpu_custom_call" | custom-call | tf_op jit(solution)/shard_map/pallas_call | solution.py:357
  96.5 2.7 %copy.9 = bf16[1,256,3072]{2,1,0:T(8,128)(2,1)} copy(bf16[1,256,3072]{2,1,0:T(8,128)(2,1)} %bitcast.6) | data formatting | bytes 3145728

commit v3 on v2

v3 whole, which is shorter than its diff:
```python
import functools
import math

import jax
import jax.numpy as jnp
from jax import lax
from jax.experimental import pallas as pl
from jax.experimental.pallas import tpu as pltpu
from jax.sharding import PartitionSpec as P

MESH = pl.DeviceIdType.MESH
CONTRACT_LAST = (((1,), (1,)), ((), ()))
LANES = 128
HOP = 2
AHEAD = 3
PIECES = 16


def kernel(
    edits, ring,
    proj, inj, text, text_len, weight, gate, out,
    queries, kv, text_kv, src, inj_own, inj_here, mask, s_a, s_b, m_a, m_b, rows_out, cols_out, weight_here,
    early_out, early_top, weight_sem, text_send, text_recv, inj_send, inj_recv, q_send, q_recv,
    cast_send, cast_recv, kv_send, kv_recv, o_send, o_recv,
):
    e = lax.axis_index("edit")
    me = lax.axis_index("seq")
    z, half = e // 2, e % 2
    depth = edits // 2
    rows = proj.shape[2]
    group = rows * ring
    root = e == 0
    swap = ring // 2
    other_row = lax.rem(me + swap, ring)

    def peer(d):
        return lax.rem(me + d, ring)

    def head_of(device):
        return lax.rem(device + swap * half, ring)

    def columns(head):
        return pl.ds(pl.multiple_of(head * LANES, LANES), LANES)

    def each(first, last, action):
        def step(d, carry):
            action(d)
            return carry

        lax.fori_loop(first, last, step, 0)

    load_weight = pltpu.make_async_copy(weight, weight_here, weight_sem)
    load_weight.start()

    barrier = pltpu.get_barrier_semaphore()

    def greet(d):
        pl.semaphore_signal(barrier, inc=1, device_id=(e, peer(d)), device_id_type=MESH)

    each(1, ring, greet)
    up, down = lax.rem(z + 1, depth), lax.rem(z + depth - 1, depth)
    for other in ((up * 2 + half, me), (down * 2 + half, me), (z * 2 + 1 - half, other_row)):
        pl.semaphore_signal(barrier, inc=1, device_id=other, device_id_type=MESH)
    inj_own[...] = jnp.zeros_like(inj_own)
    inj_own[0:1, 0:ring] = inj[...]
    for k in range(PIECES):
        kv[1, k, :, :, LANES:] = jnp.ones((ring, rows, LANES), jnp.bfloat16)
    text_kv[1, :, LANES:] = jnp.ones((group, LANES), jnp.bfloat16)
    pl.semaphore_wait(barrier, ring - 1 + 3)

    def q_copy(k, d, many):
        there = peer(d)
        return pltpu.make_async_remote_copy(
            proj.at[0, pl.ds(k, many), :, columns(head_of(there))], queries.at[pl.ds(k, many), me],
            q_send, q_recv.at[k // 2], (e, there), MESH,
        )

    def kv_copy(k, d, many):
        there = peer(d)
        return pltpu.make_async_remote_copy(
            proj.at[pl.ds(1, 2), pl.ds(k, many), :, columns(head_of(there))],
            kv.at[:, pl.ds(k, many), me, :, pl.ds(0, LANES)],
            kv_send, kv_recv.at[k], (e, there), MESH,
        )

    def push_q(k, many):
        each(1, ring, lambda d: q_copy(k, d, many).start())
        pltpu.make_async_copy(
            proj.at[0, pl.ds(k, many), :, columns(head_of(me))],
            queries.at[pl.ds(k, many), me], q_recv.at[k // 2],
        ).start()

    def push_kv(k, many):
        each(1, ring, lambda d: kv_copy(k, d, many).start())
        pltpu.make_async_copy(
            proj.at[pl.ds(1, 2), pl.ds(k, many), :, columns(head_of(me))],
            kv.at[:, pl.ds(k, many), me, :, pl.ds(0, LANES)], kv_recv.at[k],
        ).start()

    def await_kv(k, many):
        here = kv.at[:, pl.ds(k, many), :, :, pl.ds(0, LANES)]
        pltpu.make_async_copy(here, here, kv_recv.at[k]).wait()

    def await_q(k, many):
        here = queries.at[pl.ds(k, many)]
        pltpu.make_async_copy(here, here, q_recv.at[k // 2]).wait()

    def near(distance):
        return distance - 2 * (distance // (depth - 1))

    def apart(part, odd):
        if part == 0:
            return lax.rem(z - odd + depth, depth)
        return lax.rem(2 * depth - odd - z, depth)

    def lag(part, odd):
        straight = z if part == 0 else lax.rem(depth - z, depth)
        return HOP * ((1 - half) * straight + half * (odd + 1 + near(apart(part, odd))))

    def cast_sends(part, odd):
        first, second = half == 0, half == 1
        distance = apart(part, odd)
        onward = z < depth - 1 if part == 0 else z != 1
        cross = z == odd if part == 0 else z == lax.rem(depth - odd, depth)
        back = lax.rem(z + (depth - 1) * half, depth) if part == 0 else lax.rem(z + half, depth)
        ahead = up if part == 0 else down
        return (
            (jnp.logical_or(jnp.logical_and(first, onward), jnp.logical_and(second, distance <= 1)),
             (ahead * 2 + half, me)),
            (jnp.logical_or(jnp.logical_and(first, cross), jnp.logical_and(second, distance == 0)),
             (back * 2 + 1, lax.rem(me + swap * (1 - half), ring))),
        )

    def cast_copy(k, role, part, there, first):
        here = kv.at[part, k, :, :, pl.ds(0, LANES)] if first else src.at[part, k]
        return pltpu.make_async_remote_copy(
            here, src.at[part, k], cast_send.at[2 * part + role, k],
            cast_recv.at[part, k], there, MESH,
        )

    def cast_start(k, part, odd, first):
        for role, (wanted, there) in enumerate(cast_sends(part, odd)):

            @pl.when(wanted)
            def _(role=role, there=there):
                cast_copy(k, role, part, there, first).start()

    def cast_done(k, part, odd):
        for role, (wanted, there) in enumerate(cast_sends(part, odd)):

            @pl.when(wanted)
            def _(role=role, there=there):
                cast_copy(k, role, part, there, False).wait_send()

    most = HOP * depth

    text_here = text_kv.at[:, :, pl.ds(0, LANES)]
    text_copy = pltpu.make_async_remote_copy(text, text_here, text_send, text_recv, (e, other_row), MESH)
    inj_copy = pltpu.make_async_remote_copy(inj_own, inj_here, inj_send, inj_recv, (e, other_row), MESH)


    scale = math.log2(math.e) / math.sqrt(LANES)
    usable = lax.broadcasted_iota(jnp.int32, (1, group), 1) < text_len[0]
    scores, tops = (s_a, s_b), (m_a, m_b)
    early = [PIECES] + list(range(PIECES // 2))
    late = list(range(PIECES // 2, PIECES))

    def keys_of(j):
        if j == PIECES:
            return text_kv[0, :, 0:LANES]
        return kv[0, j, :, :, 0:LANES].reshape(group, LANES)

    def values_of(j):
        if j == PIECES:
            return text_kv[1]
        return kv[1, j].reshape(group, 2 * LANES)

    def choose(k):
        for part in range(2):
            kv[part, k, :, :, 0:LANES] = jnp.where(
                mask[...] == 1,
                src[part, k].astype(jnp.float32),
                kv[part, k, :, :, 0:LANES].astype(jnp.float32),
            ).astype(jnp.bfloat16)

    def choose_two(h):
        await_kv(2 * h, 2)
        choose(2 * h)
        choose(2 * h + 1)

    def o_copy(k, d):
        there = peer(d)
        return pltpu.make_async_remote_copy(
            rows_out.at[pl.ds(k, 2), there], cols_out.at[pl.ds(k, 2), :, columns(head_of(me))],
            o_send, o_recv, (e, there), MESH,
        )

    def push_o(k):
        each(1, ring, lambda d: o_copy(k, d).start())
        pltpu.make_async_copy(
            rows_out.at[pl.ds(k, 2), me], cols_out.at[pl.ds(k, 2), :, columns(head_of(me))], o_recv
        ).start()

    def attend(chunks, i, slot, first=False, last=False):
        other = 1 - slot
        if not last:
            query = queries[i].reshape(group, LANES)
        if not first:
            before = i - 1
            top = tops[other][...]
        highest, total_out = None, None
        for place, j in enumerate(chunks):
            room = slice(place * group, (place + 1) * group)
            if not last:
                s = lax.dot_general(
                    query, keys_of(j), CONTRACT_LAST, preferred_element_type=jnp.float32
                )
                if j == PIECES:
                    s = jnp.where(usable, s, -1e30)
                scores[slot][:, room] = s
                for c in range(group // LANES):
                    part = s[:, c * LANES : (c + 1) * LANES]
                    highest = part if highest is None else jnp.maximum(highest, part)
            if not first:
                p = jnp.exp2(scores[other][:, room] * scale - top[:, 0:1]).astype(jnp.bfloat16)
                part = jnp.dot(p, values_of(j), preferred_element_type=jnp.float32)
                total_out = part if total_out is None else total_out + part
        if not last:
            found = jnp.broadcast_to(jnp.max(highest, axis=1, keepdims=True) * scale, (group, LANES))
            if chunks is late:
                found = jnp.maximum(found, early_top[i])
            tops[slot][...] = found
        if not first and chunks is early:
            early_out[before] = total_out
            early_top[before] = top
        if not first and chunks is late:
            shrink = jnp.exp2(early_top[before] - top)
            values = total_out[:, :LANES] + early_out[before, :, 0:LANES] * shrink
            weights = total_out[:, LANES:] + early_out[before, :, LANES:] * shrink
            rows_out[before] = (values / weights).astype(jnp.bfloat16).reshape(ring, rows, LANES)

    opening = PIECES + most - PIECES // 2

    def early_step(h):
        @pl.when(h == 0)
        def _():
            inj_copy.wait_recv()
            text_copy.wait_recv()

            @pl.when(jnp.logical_not(root))
            def _():
                lane = lax.broadcasted_iota(jnp.int32, (1, LANES), 1)
                for owner in range(ring):
                    taken = jnp.sum(jnp.where(lane == owner, inj_here[0:1, :], 0), axis=1, keepdims=True)
                    mask[owner] = jnp.broadcast_to(taken, (rows, LANES))
                each(0, PIECES // 4, choose_two)

            @pl.when(root)
            def _():
                await_q(0, 2)

            @pl.when(jnp.logical_not(root))
            def _():
                each(0, PIECES // 4, lambda u: await_q(4 * u, 4))

            attend(early, 0, 0, first=True)

        attend(early, 2 * h + 1, 1)

        @pl.when(h < PIECES // 2 - 1)
        def _():
            @pl.when(root)
            def _():
                await_q(2 * h + 2, 2)

            attend(early, 2 * h + 2, 0)

        @pl.when(h == PIECES // 2 - 1)
        def _():
            attend(early, PIECES, 0, last=True)

    def cast_step(t, carry):
        for odd in range(2):
            for part in range(2):
                k = t - lag(part, odd)
                here = jnp.logical_and(
                    jnp.logical_and(k >= 0, k < PIECES), lax.rem(k + 2 * most, 2) == odd
                )

                @pl.when(jnp.logical_and(here, root))
                def _(k=k, part=part, odd=odd):
                    if part == 0:
                        await_kv(k, 1)
                    cast_start(k, part, odd, True)

                @pl.when(jnp.logical_and(here, jnp.logical_not(root)))
                def _(k=k, part=part, odd=odd):
                    cast_copy(k, 0, part, (e, me), False).wait_recv()
                    cast_start(k, part, odd, False)

        @pl.when(root)
        def _():
            ahead = t + AHEAD

            @pl.when(ahead < PIECES)
            def _():
                push_kv(ahead, 1)

            @pl.when(jnp.logical_and(ahead >= PIECES, ahead < PIECES + PIECES // 2))
            def _():
                push_q(2 * (ahead - PIECES), 2)

        @pl.when(jnp.logical_not(root))
        def _():
            quick = PIECES // 4

            @pl.when(t < quick)
            def _():
                push_q(4 * t, 4)

            late_by = t - quick

            @pl.when(
                jnp.logical_and(jnp.logical_and(t >= quick, t < quick + PIECES), lax.rem(t + PIECES - quick, 2) == 0)
            )
            def _():
                push_kv(late_by, 2)

        @pl.when(t >= opening)
        def _():
            early_step(t - opening)

        return carry

    @pl.when(root)
    def _():
        each(0, AHEAD, lambda k: push_kv(k, 1))

    @pl.when(half == 1)
    def _():
        inj_copy.start()
        text_copy.start()

    @pl.when(half == 0)
    def _():
        pltpu.make_async_copy(inj_own, inj_here, inj_recv).start()
        pltpu.make_async_copy(text, text_here, text_recv).start()

    lax.fori_loop(0, PIECES + most, cast_step, 0)

    @pl.when(jnp.logical_not(root))
    def _():
        each(PIECES // 4, PIECES // 2, choose_two)

    def two(h):
        attend(late, 2 * h + 1, 1)
        attend(late, 2 * h + 2, 0)
        push_o(2 * h)

    attend(late, 0, 0, first=True)
    each(0, (PIECES - 2) // 2, two)
    attend(late, PIECES - 1, 1)
    attend(late, PIECES, 0, last=True)
    push_o(PIECES - 2)
    load_weight.wait()
    pltpu.make_async_copy(cols_out, cols_out, o_recv).wait()

    wide = 512 if out.shape[1] % 512 == 0 else LANES

    joined = cols_out[...].reshape(PIECES * rows, cols_out.shape[2])

    def project(n):
        here = pl.ds(pl.multiple_of(n * wide, wide), wide)
        result = jnp.dot(joined, weight_here[:, here], preferred_element_type=jnp.float32)
        out[:, here] = (result * gate[:, here]).astype(jnp.bfloat16)

    each(0, out.shape[1] // wide, project)

    @pl.when(half == 1)
    def _():
        inj_copy.wait_send()
        text_copy.wait_send()

    def finish_piece(k):
        for odd in range(2):

            @pl.when(lax.rem(k, 2) == odd)
            def _(odd=odd):
                for part in range(2):
                    cast_done(k, part, odd)


    each(0, PIECES, finish_piece)
    others = pl.ds(0, ring - 1)
    for sent, sem in (
        (queries.at[:, others], q_send),
        (kv.at[:, :, others, :, pl.ds(0, LANES)], kv_send),
        (rows_out.at[:, others], o_send),
    ):
        pltpu.make_async_copy(sent, sent, sem).wait()


def per_device(edits, ring, projected, inject, text_kv, text_len, out_weight, gate):
    block, width = projected.shape[1], projected.shape[3]
    rows = block // PIECES
    group = rows * ring
    half_keys = (PIECES // 2 + 1) * group
    bf16, f32, i32 = jnp.bfloat16, jnp.float32, jnp.int32
    vmem = pl.BlockSpec(memory_space=pltpu.VMEM)
    far = pl.BlockSpec(memory_space=pl.ANY)
    dma = pltpu.SemaphoreType.DMA
    result = pl.pallas_call(
        functools.partial(kernel, edits, ring),
        out_shape=jax.ShapeDtypeStruct((block, out_weight.shape[1]), bf16),
        in_specs=[far, vmem, far, pl.BlockSpec(memory_space=pltpu.SMEM), far, vmem],
        out_specs=vmem,
        scratch_shapes=[
            pltpu.VMEM((PIECES, ring, rows, LANES), bf16),
            pltpu.VMEM((2, PIECES, ring, rows, 2 * LANES), bf16),
            pltpu.VMEM((2, group, 2 * LANES), bf16),
            pltpu.VMEM((2, PIECES, ring, rows, LANES), bf16),
            pltpu.VMEM((8, LANES), i32),
            pltpu.VMEM((8, LANES), i32),
            pltpu.VMEM((ring, rows, LANES), i32),
            pltpu.VMEM((group, half_keys), f32),
            pltpu.VMEM((group, half_keys), f32),
            pltpu.VMEM((group, LANES), f32),
            pltpu.VMEM((group, LANES), f32),
            pltpu.VMEM((PIECES, ring, rows, LANES), bf16),
            pltpu.VMEM((PIECES, rows, width), bf16),
            pltpu.VMEM(out_weight.shape, bf16),
            pltpu.VMEM((PIECES, group, 2 * LANES), f32),
            pltpu.VMEM((PIECES, group, LANES), f32),
            dma, dma, dma, dma, dma, dma, dma((PIECES // 2,)),
            dma((4, PIECES)), dma((2, PIECES)), dma, dma((PIECES,)), dma, dma,
        ],
        compiler_params=pltpu.CompilerParams(
            collective_id=0, has_side_effects=True, vmem_limit_bytes=56 * 2**20
        ),
    )(
        projected[0].transpose(1, 0, 2).reshape(3, PIECES, rows, width), inject[0], text_kv[0], text_len, out_weight, gate,
    )
    return result[None]


def solution(mesh):
    return jax.shard_map(
        functools.partial(per_device, mesh.shape["edit"], mesh.shape["seq"]),
        mesh=mesh,
        in_specs=(
            P("edit", "seq", None, None),
            P("edit", "seq", None),
            P("edit", None, None, "seq"),
            P("edit"),
            P(),
            P("edit", None),
        ),
        out_specs=P("edit", "seq", None),
        check_vma=False,
    )
```

time: 99.3 us -> 85.6 us (0.86); the launches traced: 99.1 us -> 84.4 us
  Pallas kernels: 95.8 us -> 81.1 us
    pallas_call x1, Pallas kernels: 95.8 us -> 81.1 us  [per_device(): pl.pallas_call(functools.partial(kernel, edits, ring), out_shape=jax.Shap...]
where the time goes in v3:
time: 85.6 us; the launch traced here: 84.4 us
  Pallas kernels  81.1 us (95%)
  local copies, waits for them, and re-layouts  2.65 us (3%)
    pallas_call x1, Pallas kernels, per_device(): pl.pallas_call(functools.partial(kernel, edits, ring), out_shape=jax.Shap...  81.1 us
    unnamed x1, local copies, waits for them, and re-layouts  2.65 us

profile of v3, /device:TPU:49, one launch (start us, length us, event | category | flops | bytes accessed | tf_op | source)
XLA Modules:
  0.0 84.4 jit_solution(2875414879647043693)
XLA Ops:
  0.7 81.1 %shard_map.64 = bf16[256,3072]{1,0:T(8,128)(2,1)} custom-call(bf16[3,16,16,2048]{3,2,1,0:T(8,128)(2,1)} %bitcast.9, s32[1,16]{1,0:T(1,128)} %bitcast.11, bf16[2,256,128]{2,1,0:T(8,128)(2,1)} %bitcast.10, s32[1]{0:T(128)S(6)} %copy.8.text_len, bf16[2048,3072]{1,0:T(8,128)(2,1)} %weight.1, f32[1,3072]{1,0:T(1,128)} %gate.1), custom_call_target="tpu_custom_call" | custom-call | tf_op jit(solution)/shard_map/pallas_call | solution.py:412
  81.8 2.7 %copy.9 = bf16[1,256,3072]{2,1,0:T(8,128)(2,1)} copy(bf16[1,256,3072]{2,1,0:T(8,128)(2,1)} %bitcast.8) | data formatting | bytes 3145728

commit v4 on v3

--- a/solution.py
+++ b/solution.py
@@ -14,12 +14,13 @@
 HOP = 2
 AHEAD = 3
 PIECES = 16
+EARLY = 8
 
 
 def kernel(
     edits, ring,
     proj, inj, text, text_len, weight, gate, out,
-    queries, kv, text_kv, src, inj_own, inj_here, mask, s_a, s_b, m_a, m_b, rows_out, cols_out, weight_here,
+    queries, kv, text_kv, src, inj_own, inj_here, mask, s_a, s_b, m_a, m_b, rows_out, cols_out, weight_here, shown, shown_sem,
     early_out, early_top, weight_sem, text_send, text_recv, inj_send, inj_recv, q_send, q_recv,
     cast_send, cast_recv, kv_send, kv_recv, o_send, o_recv,
 ):
@@ -50,7 +51,6 @@
         lax.fori_loop(first, last, step, 0)
 
     load_weight = pltpu.make_async_copy(weight, weight_here, weight_sem)
-    load_weight.start()
 
     barrier = pltpu.get_barrier_semaphore()
 
@@ -162,8 +162,8 @@
     scale = math.log2(math.e) / math.sqrt(LANES)
     usable = lax.broadcasted_iota(jnp.int32, (1, group), 1) < text_len[0]
     scores, tops = (s_a, s_b), (m_a, m_b)
-    early = [PIECES] + list(range(PIECES // 2))
-    late = list(range(PIECES // 2, PIECES))
+    early = [PIECES] + list(range(EARLY))
+    late = list(range(EARLY, PIECES))
 
     def keys_of(j):
         if j == PIECES:
@@ -192,13 +192,15 @@
         there = peer(d)
         return pltpu.make_async_remote_copy(
             rows_out.at[pl.ds(k, 2), there], cols_out.at[pl.ds(k, 2), :, columns(head_of(me))],
-            o_send, o_recv, (e, there), MESH,
+            o_send, o_recv.at[k // (PIECES // 2)], (e, there), MESH,
         )
 
     def push_o(k):
-        each(1, ring, lambda d: o_copy(k, d).start())
+        for d in range(1, ring):
+            o_copy(k, d).start()
         pltpu.make_async_copy(
-            rows_out.at[pl.ds(k, 2), me], cols_out.at[pl.ds(k, 2), :, columns(head_of(me))], o_recv
+            rows_out.at[pl.ds(k, 2), me], cols_out.at[pl.ds(k, 2), :, columns(head_of(me))],
+            o_recv.at[k // (PIECES // 2)],
         ).start()
 
     def attend(chunks, i, slot, first=False, last=False):
@@ -239,7 +241,8 @@
             weights = total_out[:, LANES:] + early_out[before, :, LANES:] * shrink
             rows_out[before] = (values / weights).astype(jnp.bfloat16).reshape(ring, rows, LANES)
 
-    opening = PIECES + most - PIECES // 2
+    last_lag = functools.reduce(jnp.maximum, [lag(part, odd) for part in range(2) for odd in range(2)])
+    opening = jnp.where(root, PIECES + most - PIECES // 2, EARLY + last_lag)
 
     def early_step(h):
         @pl.when(h == 0)
@@ -253,7 +256,7 @@
                 for owner in range(ring):
                     taken = jnp.sum(jnp.where(lane == owner, inj_here[0:1, :], 0), axis=1, keepdims=True)
                     mask[owner] = jnp.broadcast_to(taken, (rows, LANES))
-                each(0, PIECES // 4, choose_two)
+                each(0, EARLY // 2, choose_two)
 
             @pl.when(root)
             def _():
@@ -280,6 +283,13 @@
             attend(early, PIECES, 0, last=True)
 
     def cast_step(t, carry):
+        share = weight.shape[0] // (PIECES // 2)
+
+        @pl.when(jnp.logical_and(t >= PIECES // 2, t < PIECES))
+        def _():
+            some = pl.ds(pl.multiple_of((t - PIECES // 2) * share, share), share)
+            pltpu.make_async_copy(weight.at[some], weight_here.at[some], weight_sem).start()
+
         for odd in range(2):
             for part in range(2):
                 k = t - lag(part, odd)
@@ -326,7 +336,7 @@
             def _():
                 push_kv(late_by, 2)
 
-        @pl.when(t >= opening)
+        @pl.when(jnp.logical_and(t >= opening, t < opening + PIECES // 2))
         def _():
             early_step(t - opening)
 
@@ -350,31 +360,21 @@
 
     @pl.when(jnp.logical_not(root))
     def _():
-        each(PIECES // 4, PIECES // 2, choose_two)
+        each(EARLY // 2, PIECES // 2, choose_two)
 
     def two(h):
+        push_o(2 * h - 2)
         attend(late, 2 * h + 1, 1)
         attend(late, 2 * h + 2, 0)
-        push_o(2 * h)
 
     attend(late, 0, 0, first=True)
-    each(0, (PIECES - 2) // 2, two)
+    attend(late, 1, 1)
+    attend(late, 2, 0)
+    each(1, (PIECES - 2) // 2, two)
+    push_o(PIECES - 4)
     attend(late, PIECES - 1, 1)
     attend(late, PIECES, 0, last=True)
     push_o(PIECES - 2)
-    load_weight.wait()
-    pltpu.make_async_copy(cols_out, cols_out, o_recv).wait()
-
-    wide = 512 if out.shape[1] % 512 == 0 else LANES
-
-    joined = cols_out[...].reshape(PIECES * rows, cols_out.shape[2])
-
-    def project(n):
-        here = pl.ds(pl.multiple_of(n * wide, wide), wide)
-        result = jnp.dot(joined, weight_here[:, here], preferred_element_type=jnp.float32)
-        out[:, here] = (result * gate[:, here]).astype(jnp.bfloat16)
-
-    each(0, out.shape[1] // wide, project)
 
     @pl.when(half == 1)
     def _():
@@ -388,32 +388,49 @@
             def _(odd=odd):
                 for part in range(2):
                     cast_done(k, part, odd)
-
 
     each(0, PIECES, finish_piece)
     others = pl.ds(0, ring - 1)
     for sent, sem in (
         (queries.at[:, others], q_send),
         (kv.at[:, :, others, :, pl.ds(0, LANES)], kv_send),
-        (rows_out.at[:, others], o_send),
     ):
         pltpu.make_async_copy(sent, sent, sem).wait()
+    load_weight.wait()
+
+    wide = 512 if out.shape[1] % 512 == 0 else LANES
+    middle = PIECES // 2
+    for part in range(2):
+        arrived = cols_out.at[pl.ds(part * middle, middle)]
+        pltpu.make_async_copy(arrived, arrived, o_recv.at[part]).wait()
+        joined = arrived[...].reshape(middle * rows, cols_out.shape[2])
+        lines = pl.ds(part * middle * rows, middle * rows)
+
+        def project(n):
+            here = pl.ds(pl.multiple_of(n * wide, wide), wide)
+            result = jnp.dot(joined, weight_here[:, here], preferred_element_type=jnp.float32)
+            shown[lines, here] = (result * gate[:, here]).astype(jnp.bfloat16)
+            pltpu.make_async_copy(shown.at[lines, here], out.at[lines, here], shown_sem).start()
+
+        each(0, out.shape[1] // wide, project)
+    pltpu.make_async_copy(rows_out.at[:, others], rows_out.at[:, others], o_send).wait()
+    pltpu.make_async_copy(shown, out, shown_sem).wait()
 
 
 def per_device(edits, ring, projected, inject, text_kv, text_len, out_weight, gate):
     block, width = projected.shape[1], projected.shape[3]
     rows = block // PIECES
     group = rows * ring
-    half_keys = (PIECES // 2 + 1) * group
+    half_keys = max(EARLY + 1, PIECES - EARLY) * group
     bf16, f32, i32 = jnp.bfloat16, jnp.float32, jnp.int32
     vmem = pl.BlockSpec(memory_space=pltpu.VMEM)
-    far = pl.BlockSpec(memory_space=pl.ANY)
+    far = pl.BlockSpec(memory_space=pltpu.HBM)
     dma = pltpu.SemaphoreType.DMA
     result = pl.pallas_call(
         functools.partial(kernel, edits, ring),
         out_shape=jax.ShapeDtypeStruct((block, out_weight.shape[1]), bf16),
         in_specs=[far, vmem, far, pl.BlockSpec(memory_space=pltpu.SMEM), far, vmem],
-        out_specs=vmem,
+        out_specs=pl.BlockSpec(memory_space=pl.ANY),
         scratch_shapes=[
             pltpu.VMEM((PIECES, ring, rows, LANES), bf16),
             pltpu.VMEM((2, PIECES, ring, rows, 2 * LANES), bf16),
@@ -429,13 +446,15 @@
             pltpu.VMEM((PIECES, ring, rows, LANES), bf16),
             pltpu.VMEM((PIECES, rows, width), bf16),
             pltpu.VMEM(out_weight.shape, bf16),
+            pltpu.VMEM((block, out_weight.shape[1]), bf16),
+            dma,
             pltpu.VMEM((PIECES, group, 2 * LANES), f32),
             pltpu.VMEM((PIECES, group, LANES), f32),
             dma, dma, dma, dma, dma, dma, dma((PIECES // 2,)),
-            dma((4, PIECES)), dma((2, PIECES)), dma, dma((PIECES,)), dma, dma,
+            dma((4, PIECES)), dma((2, PIECES)), dma, dma((PIECES,)), dma, dma((2,)),
         ],
         compiler_params=pltpu.CompilerParams(
-            collective_id=0, has_side_effects=True, vmem_limit_bytes=56 * 2**20
+            collective_id=0, has_side_effects=True, vmem_limit_bytes=50 * 2**20
         ),
     )(
         projected[0].transpose(1, 0, 2).reshape(3, PIECES, rows, width), inject[0], text_kv[0], text_len, out_weight, gate,

time: 85.6 us -> 81 us (0.946); the launches traced: 84.4 us -> 80.8 us
  Pallas kernels: 81.1 us -> 76.7 us
    pallas_call x1, Pallas kernels: 81.1 us -> 76.7 us  [per_device(): pl.pallas_call(functools.partial(kernel, edits, ring), out_shape=jax.Shap...]
    unnamed x1 -> x7, local copies, waits for them, and re-layouts: 2.65 us -> 3.4 us
where the time goes in v4:
time: 81 us; the launch traced here: 80.8 us
  Pallas kernels  76.7 us (95%)
  local copies, waits for them, and re-layouts  3.4 us (4%)
    pallas_call x1, Pallas kernels, per_device(): pl.pallas_call(functools.partial(kernel, edits, ring), out_shape=jax.Shap...  76.7 us
    unnamed x7, local copies, waits for them, and re-layouts  3.4 us

profile of v4, /device:TPU:49, one launch (start us, length us, event | category | flops | bytes accessed | tf_op | source)
XLA Modules:
  0.0 80.8 jit_solution(6625594146066936232)
XLA Ops:
  0.7 0.0 copy-start
  0.7 0.9 %copy-done = bf16[1,2,256,128]{3,2,1,0:T(8,128)(2,1)S(1)} copy-done((bf16[1,2,256,128]{3,2,1,0:T(8,128)(2,1)S(1)}, bf16[1,2,256,128]{3,2,1,0:T(8,128)(2,1)}, u32[]{:S(2)}) %copy-start) | copy-done | bytes 131096
  1.6 0.0 copy-start.1
  1.6 0.7 copy-done.1
  2.3 0.0 copy-start.2
  2.3 0.7 copy-done.2
  2.9 76.7 %shard_map.64 = bf16[256,3072]{1,0:T(8,128)(2,1)S(1)} custom-call(bf16[3,16,16,2048]{3,2,1,0:T(8,128)(2,1)} %bitcast.11, s32[1,16]{1,0:T(1,128)S(1)} %bitcast.10, bf16[2,256,128]{2,1,0:T(8,128)(2,1)S(1)} %bitcast.9, s32[1]{0:T(128)S(6)} %copy.8.text_len, bf16[2048,3072]{1,0:T(8,128)(2,1)} %weight.1, f32[1,3072]{1,0:T(1,128)S(1)} %copy-done.1), custom_call_target="tpu_custom_call" | custom-call | tf_op jit(solution)/shard_map/pallas_call | solution.py:429
  79.7 1.1 %copy.9 = bf16[1,256,3072]{2,1,0:T(8,128)(2,1)} copy(bf16[1,256,3072]{2,1,0:T(8,128)(2,1)S(1)} %bitcast.8) | data formatting | bytes 3145728
Async XLA Ops:
  0.7 0.9 %copy-start = (bf16[1,2,256,128]{3,2,1,0:T(8,128)(2,1)S(1)}, bf16[1,2,256,128]{3,2,1,0:T(8,128)(2,1)}, u32[]{:S(2)}) copy-start(bf16[1,2,256,128]{3,2,1,0:T(8,128)(2,1)} %param.8) | copy-start | bytes 393220
  1.6 0.7 copy-start.1
  2.3 0.7 copy-start.2

commit v5 on v4

--- a/solution.py
+++ b/solution.py
@@ -398,7 +398,7 @@
         pltpu.make_async_copy(sent, sent, sem).wait()
     load_weight.wait()
 
-    wide = 512 if out.shape[1] % 512 == 0 else LANES
+    wide = 1024 if out.shape[1] % 1024 == 0 else LANES
     middle = PIECES // 2
     for part in range(2):
         arrived = cols_out.at[pl.ds(part * middle, middle)]
@@ -454,7 +454,7 @@
             dma((4, PIECES)), dma((2, PIECES)), dma, dma((PIECES,)), dma, dma((2,)),
         ],
         compiler_params=pltpu.CompilerParams(
-            collective_id=0, has_side_effects=True, vmem_limit_bytes=50 * 2**20
+            collective_id=0, has_side_effects=True, vmem_limit_bytes=52 * 2**20
         ),
     )(
         projected[0].transpose(1, 0, 2).reshape(3, PIECES, rows, width), inject[0], text_kv[0], text_len, out_weight, gate,

time: 81 us -> 80.4 us (level)
  no operation moved by 1% of the time
where the time goes in v5:
time: 80.4 us; the launch traced here: 80.2 us
  Pallas kernels  76.2 us (95%)
  local copies, waits for them, and re-layouts  3.4 us (4%)
    pallas_call x1, Pallas kernels, per_device(): pl.pallas_call(functools.partial(kernel, edits, ring), out_shape=jax.Shap...  76.2 us
    unnamed x7, local copies, waits for them, and re-layouts  3.4 us

profile of v5, /device:TPU:49, one launch (start us, length us, event | category | flops | bytes accessed | tf_op | source)
XLA Modules:
  0.0 80.2 jit_solution(16528888200194047270)
XLA Ops:
  0.7 0.0 copy-start
  0.7 0.9 %copy-done = bf16[1,2,256,128]{3,2,1,0:T(8,128)(2,1)S(1)} copy-done((bf16[1,2,256,128]{3,2,1,0:T(8,128)(2,1)S(1)}, bf16[1,2,256,128]{3,2,1,0:T(8,128)(2,1)}, u32[]{:S(2)}) %copy-start) | copy-done | bytes 131096
  1.6 0.0 copy-start.1
  1.6 0.7 copy-done.1
  2.3 0.0 copy-start.2
  2.3 0.7 copy-done.2
  2.9 76.2 %shard_map.64 = bf16[256,3072]{1,0:T(8,128)(2,1)S(1)} custom-call(bf16[3,16,16,2048]{3,2,1,0:T(8,128)(2,1)} %bitcast.11, s32[1,16]{1,0:T(1,128)S(1)} %bitcast.10, bf16[2,256,128]{2,1,0:T(8,128)(2,1)S(1)} %bitcast.9, s32[1]{0:T(128)S(6)} %copy.8.text_len, bf16[2048,3072]{1,0:T(8,128)(2,1)} %weight.1, f32[1,3072]{1,0:T(1,128)S(1)} %copy-done.1), custom_call_target="tpu_custom_call" | custom-call | tf_op jit(solution)/shard_map/pallas_call | solution.py:429
  79.1 1.1 %copy.9 = bf16[1,256,3072]{2,1,0:T(8,128)(2,1)} copy(bf16[1,256,3072]{2,1,0:T(8,128)(2,1)S(1)} %bitcast.8) | data formatting | bytes 3145728
Async XLA Ops:
  0.7 0.9 %copy-start = (bf16[1,2,256,128]{3,2,1,0:T(8,128)(2,1)S(1)}, bf16[1,2,256,128]{3,2,1,0:T(8,128)(2,1)}, u32[]{:S(2)}) copy-start(bf16[1,2,256,128]{3,2,1,0:T(8,128)(2,1)} %param.8) | copy-start | bytes 393220
  1.6 0.7 copy-start.1
  2.3 0.7 copy-start.2
